TPU v7x, 512 devices: a whole 4x8x8 slice. The times are simulated.
512 devices in a mesh: dp: 64 (over y, z), proto: 8 (over x, core).
Axes of the slice: x: 4, y: 8, z: 8, core: 2. Of those that a mesh axis runs over, the one named last changes fastest.
Arguments:
- features: bfloat16 [32768, 256], P('dp'), may hold values from -120 to 120
- prototypes: bfloat16 [256, 131072], P(None, ('proto', 'dp')), may hold values from -40 to 40
Outputs:
- row_log: float32 [32768], P('dp')
- col_log: float32 [131072], P(('proto', 'dp'))
All inputs are finite; a program needn't handle non-finite values.
Results may differ from a plain program's by a relative error of at most 0.00033.
Values may be sent and summed in bfloat16 or wider, within the bound.
A program may use at most 128 MiB of HBM per device.

v0:
```python
import jax
import jax.numpy as jnp
from jax import lax
from jax.sharding import PartitionSpec as P

K = 131072
ITERS = 3


sharpening_divisor = 0.07
epsilon_guard = 1e-06


def cluster_multiplier(piece):
    cluster_tally = piece.astype(jnp.float32)
    return (
        1.0
        / jnp.sqrt(jnp.sum(cluster_tally * cluster_tally, axis=0) + epsilon_guard)
        / sharpening_divisor
    )


def local(features, prototypes):
    rows = features.shape[0]
    image_batch = rows * lax.axis_size("dp")
    width_block = prototypes.shape[1]
    values = features.astype(jnp.float32)
    unit = (
        values / jnp.sqrt(jnp.sum(values * values, axis=1, keepdims=True) + epsilon_guard)
    ).astype(jnp.bfloat16)
    piece = lax.all_gather(prototypes, "dp", axis=1, tiled=True)
    scores = (
        jnp.dot(unit, piece, preferred_element_type=jnp.float32)
        * cluster_multiplier(piece)[None, :]
    )
    tile = jnp.exp(scores).astype(jnp.bfloat16)
    weight = jnp.ones((rows,), jnp.float32)
    own = jnp.ones((width_block,), jnp.float32)
    for step in range(ITERS):
        partial_value = jnp.sum(tile.astype(jnp.float32) * weight[:, None], axis=0)
        colsum = lax.psum(partial_value, "dp")
        colscale = 1.0 / (K * colsum)
        own = lax.dynamic_slice_in_dim(colscale, lax.axis_index("dp") * width_block, width_block, 0)
        row_part = jnp.sum(tile.astype(jnp.float32) * colscale[None, :], axis=1)
        sample_mass = lax.psum(row_part, "proto")
        weight = 1.0 / (image_batch * sample_mass)
    row_log = jnp.log(image_batch * weight)
    col_log = jnp.log(float(K) * float(image_batch) * own)
    return (row_log, col_log)


def solution(mesh):
    in_specs = (P("dp", None), P(None, ("proto", "dp")))
    out_specs = (P("dp"), P(("proto", "dp")))
    return jax.shard_map(local, mesh=mesh, in_specs=in_specs, out_specs=out_specs, check_vma=False)
```

profile of v0, /device:TPU:1, one launch (start us, length us, event | category | flops | bytes accessed | tf_op | source)
XLA Modules:
  0.0 656.5 jit_solution(13342615089492668008)
XLA Ops:
  7.2 0.7 all-gather.2.cloned.1.call-update
  7.9 0.0 all-reduce.4.cloned.1.call-start
  7.9 1.1 fusion.5
  9.1 112.2 %all-gather.2.cloned.1.call-done = bf16[256,16384]{1,0:T(8,128)(2,1)} async-done(((bf16[256,256]{1,0:T(8,128)(2,1)}), bf16[256,16384]{1,0:T(8,128)(2,1)}) %all-gather.2.cloned.1.call-update) | async-done | bytes 8388624 | tf_op jit(solution)/shard_map/all_gather | solution.py:31
  121.2 5.1 multiply_reduce_fusion
  126.4 12.5 %convert_reduce_fusion = (f32[16384]{0:T(1024)}, bf16[512,16384]{1,0:T(8,128)(2,1)}) fusion(f32[16384]{0:T(1024)S(1)} %rsqrt_multiply_fusion, bf16[256,16384]{1,0:T(8,128)(2,1)} %all-gather.2.cloned.1.call-done, bf16[512,256]{1,0:T(8,128)(2,1)} %param.2, f32[512]{0:T(512)S(1)} %add_sqrt_fusion), kind=kOutput, calls=%fused_computation.5 | convolution fusion | flops 4328898560 | bytes 25561088 | tf_op jit(solution)/shard_map/dot_general | solution.py:33
  138.9 0.0 all-reduce.6.cloned.1.call-start
  138.9 143.4 %all-reduce.4.cloned.1.call-done = f32[16384]{0:T(1024)} async-done(((f32[16384]{0:T(1024)}), f32[16384]{0:T(1024)}) %all-reduce.4.cloned.1.call-update) | async-done | bytes 65552 | tf_op jit(solution)/shard_map/psum | solution.py:41
  282.3 0.9 multiply_divide_fusion.2
  283.2 7.2 %fusion = f32[512]{0:T(512)S(1)} fusion(bf16[512,16384]{1,0:T(8,128)(2,1)} %get-tuple-element.3, f32[16384]{0:T(1024)S(1)} %multiply_divide_fusion.2), kind=kLoop, calls=%fused_computation.6 | loop fusion | flops 25165312 | bytes 16844800 | tf_op jit(solution)/shard_map/reduce_sum | solution.py:44
  290.4 17.1 %psum.43 = f32[512]{0:T(512)S(1)} all-reduce(f32[512]{0:T(512)S(1)} %fusion), channel_id=1, replica_groups=mesh['dp'=64,'proto'=8] {'proto'}, use_global_device_ids=true, to_apply=%region_5.0 | all-reduce | flops 512 | bytes 4096 | tf_op jit(solution)/shard_map/psum | solution.py:45
  307.4 8.1 %fusion.1 = f32[16384]{0:T(1024)} fusion(bf16[512,16384]{1,0:T(8,128)(2,1)} %get-tuple-element.3, f32[512]{0:T(512)S(1)} %multiply_divide_fusion.4), kind=kLoop, calls=%fused_computation.7 | loop fusion | flops 25149440 | bytes 16844800 | tf_op jit(solution)/shard_map/reduce_sum | solution.py:40
  315.6 0.0 all-reduce.8.cloned.1.call-start
  315.6 137.3 %all-reduce.6.cloned.1.call-done = f32[16384]{0:T(1024)} async-done(((f32[16384]{0:T(1024)}), f32[16384]{0:T(1024)}) %all-reduce.6.cloned.1.call-update) | async-done | bytes 65552 | tf_op jit(solution)/shard_map/psum | solution.py:41
  452.9 0.9 multiply_divide_fusion.1
  453.8 7.2 %fusion.2 = f32[512]{0:T(512)S(1)} fusion(bf16[512,16384]{1,0:T(8,128)(2,1)} %get-tuple-element.3, f32[16384]{0:T(1024)S(1)} %multiply_divide_fusion.1), kind=kLoop, calls=%fused_computation.8 | loop fusion | flops 25165312 | bytes 16844800 | tf_op jit(solution)/shard_map/reduce_sum | solution.py:44
  461.0 17.1 %psum.45 = f32[512]{0:T(512)S(1)} all-reduce(f32[512]{0:T(512)S(1)} %fusion.2), channel_id=1, replica_groups=mesh['dp'=64,'proto'=8] {'proto'}, use_global_device_ids=true, to_apply=%region_9.0 | all-reduce | flops 512 | bytes 4096 | tf_op jit(solution)/shard_map/psum | solution.py:45
  478.1 8.1 %fusion.3 = f32[16384]{0:T(1024)} fusion(bf16[512,16384]{1,0:T(8,128)(2,1)} %get-tuple-element.3, f32[512]{0:T(512)S(1)} %multiply_divide_fusion.3), kind=kLoop, calls=%fused_computation.9 | loop fusion | flops 25149440 | bytes 16844800 | tf_op jit(solution)/shard_map/reduce_sum | solution.py:40
  486.2 137.3 %all-reduce.8.cloned.1.call-done = f32[16384]{0:T(1024)} async-done(((f32[16384]{0:T(1024)}), f32[16384]{0:T(1024)}) %all-reduce.8.cloned.1.call-update) | async-done | bytes 65552 | tf_op jit(solution)/shard_map/psum | solution.py:41
  623.5 0.9 multiply_divide_fusion
  624.4 7.2 %fusion.4 = f32[512]{0:T(512)S(1)} fusion(bf16[512,16384]{1,0:T(8,128)(2,1)} %get-tuple-element.3, f32[16384]{0:T(1024)S(1)} %multiply_divide_fusion), kind=kLoop, calls=%fused_computation.10 | loop fusion | flops 25165312 | bytes 16844800 | tf_op jit(solution)/shard_map/reduce_sum | solution.py:44
  631.6 17.1 %psum.47 = f32[512]{0:T(512)S(1)} all-reduce(f32[512]{0:T(512)S(1)} %fusion.4), channel_id=1, replica_groups=mesh['dp'=64,'proto'=8] {'proto'}, use_global_device_ids=true, to_apply=%region_13.0 | all-reduce | flops 512 | bytes 4096 | tf_op jit(solution)/shard_map/psum | solution.py:45
  648.7 0.6 multiply_log_fusion
  649.3 0.6 multiply_log_fusion.1
  (8 shorter events, 0.1 us)
Async XLA Ops:
  7.2 114.1 %all-gather.2.cloned.1.call-start = ((), (), s32[]{:S(2)}) async-start(), calls=%async_computation | async-start | bytes 8519680 | tf_op jit(solution)/shard_map/all_gather | solution.py:31
  7.9 274.4 %all-reduce.4.cloned.1.call-start = ((), (), s32[]{:S(2)}) async-start(), calls=%async_computation.1 | async-start | bytes 131072 | tf_op jit(solution)/shard_map/psum | solution.py:41
  138.9 314.0 %all-reduce.6.cloned.1.call-start = ((), (), s32[]{:S(2)}) async-start(), calls=%async_computation.2 | async-start | bytes 131072 | tf_op jit(solution)/shard_map/psum | solution.py:41
  315.6 308.0 %all-reduce.8.cloned.1.call-start = ((), (), s32[]{:S(2)}) async-start(), calls=%async_computation.3 | async-start | bytes 131072 | tf_op jit(solution)/shard_map/psum | solution.py:41
Sparse Core Ops, SparseCore 0:
  11.0 110.2 all-gather.1
  139.0 143.2 all-reduce.3
  315.7 137.1 all-reduce.5
  486.3 137.1 all-reduce.7
where the time goes:
time: 657 us; the launch traced here: 656 us
  waiting for transfers between devices  531 us (81%)
  blocking collectives  51.2 us (8%)
  other arithmetic  47.9 us (7%)
  between operations  13.8 us (2%)
  matrix products  12.5 us (2%)
    psum x3, waiting for transfers between devices, local(): colsum = lax.psum(partial_value, 'dp')  418 us
    all_gather x1, waiting for transfers between devices, local(): piece = lax.all_gather(prototypes, 'dp', axis=1, tiled=True)  112 us
    psum x3, blocking collectives, local(): sample_mass = lax.psum(row_part, 'proto')  51.2 us
    reduce_sum x3, other arithmetic, local(): row_part = jnp.sum(tile.astype(jnp.float32) * colscale[None, :], axis=1)  21.6 us
    reduce_sum x2, other arithmetic, local(): partial_value = jnp.sum(tile.astype(jnp.float32) * weight[:, None], axis=0)  16.2 us
  transfers between devices with their start and end apart: 4, of which 4 were waited for; matrix products, arithmetic and copies ran while one was open for 0% of the time, Pallas kernels for 0%

commit v1 on v0

v1 whole, which is shorter than its diff:
```python
import jax
import jax.numpy as jnp
from jax import lax
from jax.experimental import pallas as pl
from jax.experimental.pallas import tpu as pltpu
from jax.sharding import PartitionSpec as P

K = 131072
IMAGES = 32768
ITERS = 3
NY = 8
NZ = 8
NP = 8
ROWS = 512
COLS = 256
HALF = ROWS // 2
LANES = 128
EPS = 1e-6
LOG2E = 1.4426950408889634
SHARP = 0.07
F32 = jnp.float32
BF16 = jnp.bfloat16
MESH = pl.DeviceIdType.MESH


def near_first(k):
    return lax.rem(jnp.where(lax.rem(k, 2) == 1, (k + 1) // 2, 8 - k // 2), 8)


def kernel(
    feat, proto, row_out, col_out,
    tile, unit, piece, scale, colacc, colbuf, colval, rowpart, rowsum, rowbuf, rowall, lastz, lastp, weight,
    unit_send, unit_recv, core_send, core_recv, piece_send, piece_recv,
    col_send, col_recv, rowp_send, rowp_recv, rowz_send, rowz_recv,
):
    dp = lax.axis_index("dp")
    me_p = lax.axis_index("proto")
    y, z = dp // NZ, lax.rem(dp, NZ)
    core = lax.rem(me_p, 2)

    def y_peer(d):
        return (lax.rem(y + d, NY) * NZ + z, me_p)

    def z_peer(d):
        return (y * NZ + lax.rem(z + d, NZ), me_p)

    def p_peer(d):
        return (dp, lax.rem(me_p + d, NP))

    other_core = (dp, me_p + 1 - 2 * core)

    barrier = pltpu.get_barrier_semaphore()

    def greet(d, _):
        pl.semaphore_signal(barrier, inc=1, device_id=y_peer(d), device_id_type=MESH)
        pl.semaphore_signal(barrier, inc=1, device_id=z_peer(d), device_id_type=MESH)
        pl.semaphore_signal(barrier, inc=1, device_id=p_peer(d), device_id_type=MESH)
        return 0

    lax.fori_loop(1, 8, greet, 0)

    values = feat[...].astype(F32)
    norm = jnp.sqrt(jnp.sum(values * values, axis=1, keepdims=True) + EPS)
    unit[pl.ds(z, 1)] = (values / norm).astype(BF16)[None]
    piece[pl.ds(y, 1)] = proto[...][None]
    colacc[...] = jnp.zeros_like(colacc)

    pl.semaphore_wait(barrier, 21)

    half = pl.ds(pl.multiple_of(core * HALF, HALF), HALF)

    def piece_copy(d):
        return pltpu.make_async_remote_copy(
            src_ref=piece.at[y], dst_ref=piece.at[y], send_sem=piece_send.at[d], recv_sem=piece_recv.at[d],
            device_id=y_peer(d), device_id_type=MESH)

    def unit_copy(d):
        return pltpu.make_async_remote_copy(
            src_ref=unit.at[z, half], dst_ref=unit.at[z, half], send_sem=unit_send.at[d], recv_sem=unit_recv.at[d],
            device_id=z_peer(d), device_id_type=MESH)

    def core_copy(d):
        source = lax.rem(z - d + NZ, NZ)
        return pltpu.make_async_remote_copy(
            src_ref=unit.at[source, half], dst_ref=unit.at[source, half],
            send_sem=core_send.at[d], recv_sem=core_recv.at[d],
            device_id=other_core, device_id_type=MESH)

    def start(k, _):
        d = near_first(k)
        unit_copy(d).start()
        piece_copy(d).start()
        return 0

    lax.fori_loop(1, 8, start, 0)

    def block(us, vs):
        scores = jnp.dot(unit[us], piece[vs], preferred_element_type=F32) * scale[vs]
        e = jnp.exp2(scores)
        tile[vs, pl.ds(pl.multiple_of(us * ROWS, ROWS), ROWS), :] = e
        colacc[vs] += jnp.sum(e.reshape(ROWS // 8, 8, COLS), axis=0)

    def arrive(k, _):
        d = near_first(k)

        @pl.when(k > 0)
        def _():
            unit_copy(d).wait_recv()
            core_copy(d).start()
            piece_copy(d).wait_recv()

        vs = lax.rem(y - d + NY, NY)
        v = piece[vs].astype(F32)
        scale[vs] = (LOG2E / SHARP) / jnp.sqrt(jnp.sum(v * v, axis=0, keepdims=True) + EPS)

        @pl.when(k > 0)
        def _():
            core_copy(d).wait_recv()

        def pair(t, _):
            ku = jnp.where(t <= k, k, t - k - 1)
            kv = jnp.where(t <= k, t, k)
            block(lax.rem(z - near_first(ku) + NZ, NZ), lax.rem(y - near_first(kv) + NY, NY))
            return 0

        lax.fori_loop(0, 2 * k + 1, pair, 0)
        return 0

    lax.fori_loop(0, 8, arrive, 0)

    def col_copy(step, d):
        return pltpu.make_async_remote_copy(
            src_ref=colbuf.at[step, y], dst_ref=colbuf.at[step, y],
            send_sem=col_send.at[step, d], recv_sem=col_recv.at[step, d],
            device_id=y_peer(d), device_id_type=MESH)

    def rowp_copy(step, d):
        return pltpu.make_async_remote_copy(
            src_ref=rowbuf.at[step, me_p], dst_ref=rowbuf.at[step, me_p],
            send_sem=rowp_send.at[step, d], recv_sem=rowp_recv.at[step, d],
            device_id=p_peer(d), device_id_type=MESH)

    def rowz_copy(step, d):
        return pltpu.make_async_remote_copy(
            src_ref=rowall.at[step, z], dst_ref=rowall.at[step, z],
            send_sem=rowz_send.at[step, d], recv_sem=rowz_recv.at[step, d],
            device_id=z_peer(d), device_id_type=MESH)

    def lastz_copy(d):
        return pltpu.make_async_remote_copy(
            src_ref=rowpart.at[lax.rem(z + d, NZ)], dst_ref=lastz.at[z],
            send_sem=rowz_send.at[ITERS - 1, d], recv_sem=rowz_recv.at[ITERS - 1, d],
            device_id=z_peer(d), device_id_type=MESH)

    def lastp_copy(d):
        return pltpu.make_async_remote_copy(
            src_ref=lastp.at[me_p], dst_ref=lastp.at[me_p],
            send_sem=rowp_send.at[ITERS - 1, d], recv_sem=rowp_recv.at[ITERS - 1, d],
            device_id=p_peer(d), device_id_type=MESH)

    def exchange(copy):
        for d in range(1, 8):
            copy(d).start()
        for d in range(1, 8):
            copy(d).wait_recv()

    def column_pass():
        def body(i, acc):
            rows = pl.ds(pl.multiple_of(i * LANES, LANES), LANES)
            w = jnp.broadcast_to(weight[pl.ds(i, 1), :], (LANES, LANES)).T
            out = []
            for j in range(2 * NY):
                t = tile[j // 2, rows, (j % 2) * LANES:(j % 2 + 1) * LANES] * w
                out.append(acc[j] + jnp.sum(t.reshape(LANES // 8, 8, LANES), axis=0))
            return tuple(out)

        acc = lax.fori_loop(0, NZ * ROWS // LANES, body, tuple(jnp.zeros((8, LANES), F32) for _ in range(2 * NY)))
        for j in range(2 * NY):
            colacc[j // 2, :, (j % 2) * LANES:(j % 2 + 1) * LANES] = acc[j]

    def row_pass():
        def body(i, _):
            rows = pl.ds(pl.multiple_of(i * LANES, LANES), LANES)
            acc = None
            for j in range(2 * NY):
                lanes = slice((j % 2) * LANES, (j % 2 + 1) * LANES)
                t = tile[j // 2, rows, lanes] * colval[j // 2:j // 2 + 1, lanes]
                acc = t if acc is None else acc + t
            rowpart[i // 4, pl.ds(lax.rem(i, 4), 1), :] = jnp.sum(acc.T, axis=0, keepdims=True)
            return 0

        lax.fori_loop(0, NZ * ROWS // LANES, body, 0)

    for step in range(ITERS):
        if step > 0:
            column_pass()
        colbuf[step, pl.ds(y, 1)] = jnp.sum(colacc[...], axis=1)[None]
        exchange(lambda d: col_copy(step, d))
        colval[...] = 1.0 / (K * jnp.sum(colbuf[step], axis=0))
        row_pass()
        if step < ITERS - 1:
            rowbuf[step, pl.ds(me_p, 1)] = rowpart[...][None]
            exchange(lambda d: rowp_copy(step, d))
            rowall[step, pl.ds(z, 1)] = jnp.sum(rowbuf[step], axis=0)[None]
            exchange(lambda d: rowz_copy(step, d))
            w = 1.0 / (IMAGES * jnp.sum(rowall[step], axis=0))
            for i in range(NZ):
                weight[4 * i:4 * i + 4, :] = w[i]
        else:
            lastz[pl.ds(z, 1)] = rowpart[pl.ds(z, 1)]
            exchange(lastz_copy)
            lastp[pl.ds(me_p, 1)] = jnp.sum(lastz[...], axis=0)[None]
            exchange(lastp_copy)
            row_out[...] = jnp.log(IMAGES * (1.0 / (IMAGES * jnp.sum(lastp[...], axis=0))))
            col_out[...] = jnp.log(float(K) * float(IMAGES) * colval[pl.ds(y, 1), :])

    def drain(d, _):
        unit_copy(d).wait_send()
        piece_copy(d).wait_send()
        core_copy(d).wait_send()
        for step in range(ITERS):
            col_copy(step, d).wait_send()
            if step < ITERS - 1:
                rowp_copy(step, d).wait_send()
                rowz_copy(step, d).wait_send()
        lastz_copy(d).wait_send()
        lastp_copy(d).wait_send()
        return 0

    lax.fori_loop(1, 8, drain, 0)


def local(features, prototypes):
    vmem = pl.BlockSpec(memory_space=pltpu.VMEM)
    row_log, col_log = pl.pallas_call(
        kernel,
        out_shape=(
            jax.ShapeDtypeStruct((ROWS // LANES, LANES), F32),
            jax.ShapeDtypeStruct((1, COLS), F32),
        ),
        in_specs=[vmem, vmem],
        out_specs=(vmem, vmem),
        scratch_shapes=[
            pltpu.VMEM((NY, NZ * ROWS, COLS), F32),
            pltpu.VMEM((NZ, ROWS, 256), BF16),
            pltpu.VMEM((NY, 256, COLS), BF16),
            pltpu.VMEM((NY, 1, COLS), F32),
            pltpu.VMEM((NY, 8, COLS), F32),
            pltpu.VMEM((ITERS, NY, NY, COLS), F32),
            pltpu.VMEM((NY, COLS), F32),
            pltpu.VMEM((NZ, 4, LANES), F32),
            pltpu.VMEM((NZ, 4, LANES), F32),
            pltpu.VMEM((ITERS - 1, NP, NZ, 4, LANES), F32),
            pltpu.VMEM((ITERS - 1, NZ, NZ, 4, LANES), F32),
            pltpu.VMEM((NZ, 4, LANES), F32),
            pltpu.VMEM((NP, 4, LANES), F32),
            pltpu.VMEM((NZ * 4, LANES), F32),
        ]
        + [pltpu.SemaphoreType.DMA((8,))] * 6
        + [pltpu.SemaphoreType.DMA((ITERS, 8))] * 6,
        compiler_params=pltpu.CompilerParams(
            collective_id=0, has_side_effects=True, vmem_limit_bytes=56 * 2**20
        ),
        cost_estimate=pl.CostEstimate(
            flops=2 * 4096 * 2048 * 256, bytes_accessed=2**20, transcendentals=4096 * 2048
        ),
        name="sinkhorn",
    )(features, prototypes)
    return row_log.reshape(ROWS), col_log.reshape(COLS)


def solution(mesh):
    in_specs = (P("dp", None), P(None, ("proto", "dp")))
    out_specs = (P("dp"), P(("proto", "dp")))
    return jax.shard_map(local, mesh=mesh, in_specs=in_specs, out_specs=out_specs, check_vma=False)
```

time: 657 us -> 127 us (0.19)
  waiting for transfers between devices: 531 us -> 0 us
  Pallas kernels: 0 us -> 124 us
  blocking collectives: 51.2 us -> 0 us
  other arithmetic: 47.9 us -> 0 us
  between operations: 13.8 us -> 0.65 us
  matrix products: 12.5 us -> 0 us
    psum x3 -> x0, waiting for transfers between devices: 418 us -> none  [local(): colsum = lax.psum(partial_value, 'dp')]
    pallas_call x0 -> x1, Pallas kernels: none -> 124 us  [local(): pl.pallas_call(kernel, out_shape=(jax.ShapeDtypeStruct((ROWS // LANES, LA...]
    all_gather x1 -> x0, waiting for transfers between devices: 112 us -> none  [local(): piece = lax.all_gather(prototypes, 'dp', axis=1, tiled=True)]
    psum x3 -> x0, blocking collectives: 51.2 us -> none  [local(): sample_mass = lax.psum(row_part, 'proto')]
    reduce_sum x7 -> x0, other arithmetic: 44 us -> none  [the longest x3 21.6 us: local(): row_part = jnp.sum(tile.astype(jnp.float32) * colscale[None, :], axis=1)]
    dot_general x1 -> x0, matrix products: 12.5 us -> none  [local(): jnp.dot(unit, piece, preferred_element_type=jnp.float32)]
  transfers between devices with their start and end apart: 4 -> 0, of which waited for: 4 -> 0; matrix products, arithmetic and copies ran while one was open for 0% -> 0% of each run, Pallas kernels for 0% -> 0%
where the time goes in v1:
time: 127 us; the launch traced here: 126 us
  Pallas kernels  124 us (98%)
  local copies, waits for them, and re-layouts  1.86 us (1%)
    pallas_call x1, Pallas kernels, local(): pl.pallas_call(kernel, out_shape=(jax.ShapeDtypeStruct((ROWS // LANES, LA...  124 us

profile of v1, /device:TPU:1, one launch (start us, length us, event | category | flops | bytes accessed | tf_op | source)
XLA Modules:
  0.0 126.4 jit_solution(13636557302619576516)
XLA Ops:
  0.6 123.9 %sinkhorn.1 = (f32[4,128]{1,0:T(4,128)}, f32[1,256]{1,0:T(1,128)}) custom-call(bf16[512,256]{1,0:T(8,128)(2,1)} %feat.1, bf16[256,256]{1,0:T(8,128)(2,1)} %proto.1), custom_call_target="tpu_custom_call" | custom-call | flops 4294967296 | bytes 1048576 | tf_op jit(solution)/shard_map/sinkhorn/pallas_call | solution.py:235
  124.5 0.0 copy-start
  124.5 0.7 copy-done
  125.2 0.0 copy-start.1
  125.2 0.6 copy.6
  125.7 0.1 copy-done.1
  125.8 0.6 copy.7
Async XLA Ops:
  124.5 0.7 copy-start
  125.2 0.6 copy-start.1

commit v2 on v1

v2 whole, which is shorter than its diff:
```python
import jax
import jax.numpy as jnp
from jax import lax
from jax.experimental import pallas as pl
from jax.experimental.pallas import tpu as pltpu
from jax.sharding import PartitionSpec as P

K = 131072
IMAGES = 32768
ITERS = 3
NY = 8
NZ = 8
NP = 8
ROWS = 512
COLS = 256
HALF = ROWS // 2
CHUNKS = 2
BLOCK = 512
NBLOCK = NZ * ROWS // BLOCK
PER = BLOCK // 128
LANES = 128
EPS = 1e-6
LOG2E = 1.4426950408889634
SHARP = 0.07
F32 = jnp.float32
BF16 = jnp.bfloat16
MESH = pl.DeviceIdType.MESH


def near_first(k):
    return lax.rem(jnp.where(lax.rem(k, 2) == 1, (k + 1) // 2, 8 - k // 2), 8)


def kernel(
    feat, proto, row_out, col_out,
    tile, unit, piece, scale, colacc, colbuf, colval, rowpart, rowbuf, rowall, lastz, lastp, weight, wide,
    unit_send, unit_recv, core_send, core_recv, piece_send, piece_recv,
    col_send, col_recv, rowp_send, rowp_recv, rowz_send, rowz_recv, wcore_send, wcore_recv,
):
    dp = lax.axis_index("dp")
    me_p = lax.axis_index("proto")
    y, z = dp // NZ, lax.rem(dp, NZ)
    core = lax.rem(me_p, 2)

    def y_peer(d):
        return (lax.rem(y + d, NY) * NZ + z, me_p)

    def z_peer(d):
        return (y * NZ + lax.rem(z + d, NZ), me_p)

    def p_peer(d):
        return (dp, lax.rem(me_p + d, NP))

    other_core = (dp, me_p + 1 - 2 * core)

    barrier = pltpu.get_barrier_semaphore()

    def greet(d, _):
        pl.semaphore_signal(barrier, inc=1, device_id=y_peer(d), device_id_type=MESH)
        pl.semaphore_signal(barrier, inc=1, device_id=z_peer(d), device_id_type=MESH)
        pl.semaphore_signal(barrier, inc=1, device_id=p_peer(d), device_id_type=MESH)
        return 0

    lax.fori_loop(1, 8, greet, 0)

    values = feat[...].astype(F32)
    norm = jnp.sqrt(jnp.sum(values * values, axis=1, keepdims=True) + EPS)
    unit[pl.ds(z, 1)] = (values / norm).astype(BF16)[None]
    piece[pl.ds(y, 1)] = proto[...][None]
    colacc[...] = jnp.zeros_like(colacc)

    def set_scale(vs):
        v = piece[vs].astype(F32)
        scale[vs] = (LOG2E / SHARP) / jnp.sqrt(jnp.sum(v * v, axis=0, keepdims=True) + EPS)

    set_scale(y)
    pl.semaphore_wait(barrier, 21)

    def chunk(c):
        return pl.ds(c * (256 // CHUNKS), 256 // CHUNKS)

    def half_chunk(c):
        rows = 256 // CHUNKS
        return pl.ds(pl.multiple_of(core * HALF + c * rows, rows), rows)

    def way(r):
        return 1 if r == 0 else 7

    def piece_copy(r, s, c):
        slot = lax.rem(y + 8 * (s - 1) - way(r) * (s - 1), NY)
        return pltpu.make_async_remote_copy(
            src_ref=piece.at[slot, chunk(c)], dst_ref=piece.at[slot, chunk(c)],
            send_sem=piece_send.at[r, s, c], recv_sem=piece_recv.at[r, s, c],
            device_id=y_peer(way(r)), device_id_type=MESH)

    def unit_copy(r, s, c):
        slot = lax.rem(z + 8 * (s - 1) - way(r) * (s - 1), NZ)
        return pltpu.make_async_remote_copy(
            src_ref=unit.at[slot, half_chunk(c)], dst_ref=unit.at[slot, half_chunk(c)],
            send_sem=unit_send.at[r, s, c], recv_sem=unit_recv.at[r, s, c],
            device_id=z_peer(way(r)), device_id_type=MESH)

    def core_copy(r, s, c):
        slot = lax.rem(z + 8 * s - way(r) * s, NZ)
        return pltpu.make_async_remote_copy(
            src_ref=unit.at[slot, half_chunk(c)], dst_ref=unit.at[slot, half_chunk(c)],
            send_sem=core_send.at[r, s, c], recv_sem=core_recv.at[r, s, c],
            device_id=other_core, device_id_type=MESH)

    for c in range(CHUNKS):
        for r in range(2):
            unit_copy(r, 1, c).start()
            piece_copy(r, 1, c).start()

    def slot_pair(t):
        k = sum((t >= j * j).astype(jnp.int32) for j in range(1, 8))
        rest = t - k * k
        ku = jnp.where(rest <= k, k, rest - k - 1)
        kv = jnp.where(rest <= k, rest, k)
        return lax.rem(z - near_first(ku) + NZ, NZ), lax.rem(y - near_first(kv) + NY, NY)

    def four(b, _):
        for q in range(4):
            us, vs = slot_pair(4 * b + q)
            e = jnp.exp2(jnp.dot(unit[us], piece[vs], preferred_element_type=F32) * scale[vs])
            tile[vs, pl.ds(pl.multiple_of(us * ROWS, ROWS), ROWS), :] = e
            colacc[vs] += jnp.sum(e.reshape(ROWS // 8, 8, COLS), axis=0)
        return 0

    def arrive(s, _):
        for c in range(CHUNKS):
            for r in range(2):
                @pl.when(s + r <= 4)
                def _():
                    unit_copy(r, s, c).wait_recv()
                    core_copy(r, s, c).start()

                    @pl.when(s + r < 4)
                    def _():
                        unit_copy(r, s + 1, c).start()

                    piece_copy(r, s, c).wait_recv()

                    @pl.when(s + r < 4)
                    def _():
                        piece_copy(r, s + 1, c).start()

        set_scale(lax.rem(y + 7 * s, NY))

        @pl.when(s < 4)
        def _():
            set_scale(lax.rem(y + s, NY))

        for c in range(CHUNKS):
            for r in range(2):
                @pl.when(s + r <= 4)
                def _():
                    core_copy(r, s, c).wait_recv()

        before = 2 * s - 1
        now = jnp.minimum(2 * s + 1, 8)
        lax.fori_loop(before * before // 4, now * now // 4, four, 0)
        return 0

    lax.fori_loop(1, 5, arrive, 0)

    def col_copy(step, d):
        return pltpu.make_async_remote_copy(
            src_ref=colbuf.at[step, y], dst_ref=colbuf.at[step, y],
            send_sem=col_send.at[step, d], recv_sem=col_recv.at[step, d],
            device_id=y_peer(d), device_id_type=MESH)

    def rowp_copy(step, d):
        target = lax.rem(me_p + d, NP)
        return pltpu.make_async_remote_copy(
            src_ref=rowpart.at[pl.ds(4 * lax.rem(target, 2), 4)], dst_ref=rowbuf.at[step, me_p],
            send_sem=rowp_send.at[step, d], recv_sem=rowp_recv.at[step, d],
            device_id=p_peer(d), device_id_type=MESH)

    def rowz_copy(step, d):
        return pltpu.make_async_remote_copy(
            src_ref=rowall.at[step, z], dst_ref=rowall.at[step, z],
            send_sem=rowz_send.at[step, d], recv_sem=rowz_recv.at[step, d],
            device_id=z_peer(d), device_id_type=MESH)

    def weight_copy(step):
        return pltpu.make_async_remote_copy(
            src_ref=weight.at[step, core], dst_ref=weight.at[step, core],
            send_sem=wcore_send.at[step], recv_sem=wcore_recv.at[step],
            device_id=other_core, device_id_type=MESH)

    def lastz_copy(d):
        return pltpu.make_async_remote_copy(
            src_ref=rowpart.at[lax.rem(z + d, NZ)], dst_ref=lastz.at[z],
            send_sem=rowz_send.at[ITERS - 1, d], recv_sem=rowz_recv.at[ITERS - 1, d],
            device_id=z_peer(d), device_id_type=MESH)

    def lastp_copy(d):
        return pltpu.make_async_remote_copy(
            src_ref=lastp.at[me_p], dst_ref=lastp.at[me_p],
            send_sem=rowp_send.at[ITERS - 1, d], recv_sem=rowp_recv.at[ITERS - 1, d],
            device_id=p_peer(d), device_id_type=MESH)

    def exchange(copy):
        for d in range(1, 8):
            copy(d).start()
        for d in range(1, 8):
            copy(d).wait_recv()

    def rows_of(i, q):
        return pl.ds(pl.multiple_of(i * BLOCK + q * LANES, LANES), LANES)

    def column_pass(step):
        def spread(h, i):
            return [jnp.broadcast_to(weight[step, h, pl.ds(i * PER + q, 1), :], (LANES, LANES)).T for q in range(PER)]

        def half_pass(h, acc):
            first = h * (NBLOCK // 2)
            for q, w in enumerate(spread(h, 0)):
                wide[0, q] = w

            def body(i, acc):
                acc = list(acc)
                ws = [wide[lax.rem(i, 2), q] for q in range(PER)]
                ahead = spread(h, jnp.minimum(i + 1, NBLOCK // 2 - 1))
                for q in range(PER):
                    for j in range(2 * NY):
                        t = tile[j // 2, rows_of(first + i, q), (j % 2) * LANES:(j % 2 + 1) * LANES] * ws[q]
                        acc[j] = acc[j] + jnp.sum(t.reshape(LANES // 8, 8, LANES), axis=0)
                for q in range(PER):
                    wide[1 - lax.rem(i, 2), q] = ahead[q]
                return tuple(acc)

            return lax.fori_loop(0, NBLOCK // 2, body, acc)

        acc = half_pass(core, tuple(jnp.zeros((8, LANES), F32) for _ in range(2 * NY)))
        weight_copy(step).wait_recv()
        acc = half_pass(1 - core, acc)
        for j in range(2 * NY):
            colacc[j // 2, :, (j % 2) * LANES:(j % 2 + 1) * LANES] = acc[j]

    def row_pass():
        def work(i):
            out = []
            for q in range(PER):
                acc = None
                for j in range(2 * NY):
                    lanes = slice((j % 2) * LANES, (j % 2 + 1) * LANES)
                    t = tile[j // 2, rows_of(i, q), lanes] * colval[j // 2:j // 2 + 1, lanes]
                    acc = t if acc is None else acc + t
                out.append(acc)
            return out

        def finish(i):
            return [jnp.sum(wide[lax.rem(i, 2), q].T, axis=0, keepdims=True) for q in range(PER)]

        def put(i, sums):
            for q in range(PER):
                n = i * PER + q
                rowpart[n // 4, pl.ds(lax.rem(n, 4), 1), :] = sums[q]

        for q, part in enumerate(work(0)):
            wide[0, q] = part

        def body(i, _):
            sums = finish(i - 1)
            parts = work(i)
            put(i - 1, sums)
            for q in range(PER):
                wide[lax.rem(i, 2), q] = parts[q]
            return 0

        lax.fori_loop(1, NBLOCK, body, 0)
        put(NBLOCK - 1, finish(NBLOCK - 1))

    for step in range(ITERS):
        if step > 0:
            column_pass(step - 1)
        colbuf[step, pl.ds(y, 1)] = jnp.sum(colacc[...], axis=1)[None]
        exchange(lambda d: col_copy(step, d))
        colval[...] = 1.0 / (K * jnp.sum(colbuf[step], axis=0))
        row_pass()
        if step < ITERS - 1:
            rowbuf[step, pl.ds(me_p, 1)] = rowpart[pl.ds(4 * core, 4)][None]
            exchange(lambda d: rowp_copy(step, d))
            rowall[step, pl.ds(z, 1)] = jnp.sum(rowbuf[step], axis=0)[None]
            exchange(lambda d: rowz_copy(step, d))
            w = 1.0 / (IMAGES * jnp.sum(rowall[step], axis=0))
            for i in range(4):
                weight[step, core, 4 * i:4 * i + 4, :] = w[i]
            weight_copy(step).start()
            for d in range(1, 8):
                rowp_copy(step, d).wait_send()
        else:
            lastz[pl.ds(z, 1)] = rowpart[pl.ds(z, 1)]
            exchange(lastz_copy)
            lastp[pl.ds(me_p, 1)] = jnp.sum(lastz[...], axis=0)[None]
            exchange(lastp_copy)
            row_out[...] = jnp.log(IMAGES * (1.0 / (IMAGES * jnp.sum(lastp[...], axis=0))))
            col_out[...] = jnp.log(float(K) * float(IMAGES) * colval[pl.ds(y, 1), :])

    for r in range(2):
        for c in range(CHUNKS):
            def drain_ring(s, _):
                unit_copy(r, s, c).wait_send()
                piece_copy(r, s, c).wait_send()
                core_copy(r, s, c).wait_send()
                return 0

            lax.fori_loop(1, 5 - r, drain_ring, 0)
    for step in range(ITERS - 1):
        weight_copy(step).wait_send()

    def drain(d, _):
        for step in range(ITERS):
            col_copy(step, d).wait_send()
            if step < ITERS - 1:
                rowz_copy(step, d).wait_send()
        lastz_copy(d).wait_send()
        lastp_copy(d).wait_send()
        return 0

    lax.fori_loop(1, 8, drain, 0)


def local(features, prototypes):
    vmem = pl.BlockSpec(memory_space=pltpu.VMEM)
    row_log, col_log = pl.pallas_call(
        kernel,
        out_shape=(
            jax.ShapeDtypeStruct((ROWS // LANES, LANES), F32),
            jax.ShapeDtypeStruct((1, COLS), F32),
        ),
        in_specs=[vmem, vmem],
        out_specs=(vmem, vmem),
        scratch_shapes=[
            pltpu.VMEM((NY, NZ * ROWS, COLS), F32),
            pltpu.VMEM((NZ, ROWS, 256), BF16),
            pltpu.VMEM((NY, 256, COLS), BF16),
            pltpu.VMEM((NY, 1, COLS), F32),
            pltpu.VMEM((NY, 8, COLS), F32),
            pltpu.VMEM((ITERS, NY, NY, COLS), F32),
            pltpu.VMEM((NY, COLS), F32),
            pltpu.VMEM((NZ, 4, LANES), F32),
            pltpu.VMEM((ITERS - 1, NP, 4, 4, LANES), F32),
            pltpu.VMEM((ITERS - 1, NZ, 4, 4, LANES), F32),
            pltpu.VMEM((NZ, 4, LANES), F32),
            pltpu.VMEM((NP, 4, LANES), F32),
            pltpu.VMEM((ITERS - 1, 2, NZ * 2, LANES), F32),
            pltpu.VMEM((2, PER, LANES, LANES), F32),
        ]
        + [pltpu.SemaphoreType.DMA((2, 5, CHUNKS))] * 6
        + [pltpu.SemaphoreType.DMA((ITERS, 8))] * 6
        + [pltpu.SemaphoreType.DMA((ITERS - 1,))] * 2,
        compiler_params=pltpu.CompilerParams(
            collective_id=0, has_side_effects=True, vmem_limit_bytes=56 * 2**20
        ),
        cost_estimate=pl.CostEstimate(
            flops=2 * 4096 * 2048 * 256, bytes_accessed=2**20, transcendentals=4096 * 2048
        ),
        name="sinkhorn",
    )(features, prototypes)
    return row_log.reshape(ROWS), col_log.reshape(COLS)


def solution(mesh):
    in_specs = (P("dp", None), P(None, ("proto", "dp")))
    out_specs = (P("dp"), P(("proto", "dp")))
    return jax.shard_map(local, mesh=mesh, in_specs=in_specs, out_specs=out_specs, check_vma=False)
```

time: 127 us -> 98.3 us (0.77)
  Pallas kernels: 124 us -> 95.6 us
    pallas_call x1, Pallas kernels: 124 us -> 95.6 us  [local(): pl.pallas_call(kernel, out_shape=(jax.ShapeDtypeStruct((ROWS // LANES, LA...]
where the time goes in v2:
time: 98.3 us; the launch traced here: 98.1 us
  Pallas kernels  95.6 us (97%)
  local copies, waits for them, and re-layouts  1.86 us (2%)
    pallas_call x1, Pallas kernels, local(): pl.pallas_call(kernel, out_shape=(jax.ShapeDtypeStruct((ROWS // LANES, LA...  95.6 us

profile of v2, /device:TPU:1, one launch (start us, length us, event | category | flops | bytes accessed | tf_op | source)
XLA Modules:
  0.0 98.1 jit_solution(12195051949383060558)
XLA Ops:
  0.6 95.6 %sinkhorn.1 = (f32[4,128]{1,0:T(4,128)}, f32[1,256]{1,0:T(1,128)}) custom-call(bf16[512,256]{1,0:T(8,128)(2,1)} %feat.1, bf16[256,256]{1,0:T(8,128)(2,1)} %proto.1), custom_call_target="tpu_custom_call" | custom-call | flops 4294967296 | bytes 1048576 | tf_op jit(solution)/shard_map/sinkhorn/pallas_call | solution.py:328
  96.3 0.0 copy-start
  96.3 0.7 copy-done
  96.9 0.0 copy-start.1
  96.9 0.6 copy.6
  97.5 0.1 copy-done.1
  97.6 0.6 copy.7
Async XLA Ops:
  96.3 0.7 copy-start
  96.9 0.6 copy-start.1

commit v3 on v2

v3 whole, which is shorter than its diff:
```python
import jax
import jax.numpy as jnp
from jax import lax
from jax.experimental import pallas as pl
from jax.experimental.pallas import tpu as pltpu
from jax.sharding import PartitionSpec as P

K = 131072
IMAGES = 32768
ITERS = 3
NY = 8
NZ = 8
NP = 8
ROWS = 512
COLS = 256
HALF = ROWS // 2
CHUNKS = 2
SPLIT = 4
PART = NZ // SPLIT
FAR_FIRST = (4, 3, 5, 2, 6, 1, 7)
BLOCK = 512
NBLOCK = NZ * ROWS // BLOCK
PER = BLOCK // 128
LANES = 128
EPS = 1e-6
LOG2E = 1.4426950408889634
SHARP = 0.07
F32 = jnp.float32
BF16 = jnp.bfloat16
MESH = pl.DeviceIdType.MESH


def near_first(k):
    return lax.rem(jnp.where(lax.rem(k, 2) == 1, (k + 1) // 2, 8 - k // 2), 8)


def kernel(
    feat, proto, row_out, col_out,
    tile, unit, piece, scale, colacc, colbuf, colval, rowpart, rowbuf, rowall, lastz, lastp, weight, wide,
    unit_send, unit_recv, core_send, core_recv, piece_send, piece_recv,
    col_send, col_recv, rowp_send, rowp_recv, rowz_send, rowz_recv,
):
    dp = lax.axis_index("dp")
    me_p = lax.axis_index("proto")
    y, z = dp // NZ, lax.rem(dp, NZ)
    core = lax.rem(me_p, 2)

    def y_peer(d):
        return (lax.rem(y + d, NY) * NZ + z, me_p)

    def z_peer(d):
        return (y * NZ + lax.rem(z + d, NZ), me_p)

    def p_peer(d):
        return (dp, lax.rem(me_p + d, NP))

    other_core = (dp, me_p + 1 - 2 * core)

    barrier = pltpu.get_barrier_semaphore()

    def greet(d, _):
        pl.semaphore_signal(barrier, inc=1, device_id=y_peer(d), device_id_type=MESH)
        pl.semaphore_signal(barrier, inc=1, device_id=z_peer(d), device_id_type=MESH)
        pl.semaphore_signal(barrier, inc=1, device_id=p_peer(d), device_id_type=MESH)
        return 0

    lax.fori_loop(1, 8, greet, 0)

    values = feat[...].astype(F32)
    norm = jnp.sqrt(jnp.sum(values * values, axis=1, keepdims=True) + EPS)
    unit[pl.ds(z, 1)] = (values / norm).astype(BF16)[None]
    piece[pl.ds(y, 1)] = proto[...][None]
    colacc[...] = jnp.zeros_like(colacc)

    def set_scale(vs):
        v = piece[vs].astype(F32)
        scale[vs] = (LOG2E / SHARP) / jnp.sqrt(jnp.sum(v * v, axis=0, keepdims=True) + EPS)

    set_scale(y)
    pl.semaphore_wait(barrier, 21)

    def chunk(c):
        return pl.ds(c * (256 // CHUNKS), 256 // CHUNKS)

    def half_chunk(c):
        rows = 256 // CHUNKS
        return pl.ds(pl.multiple_of(core * HALF + c * rows, rows), rows)

    def way(r):
        return 1 if r == 0 else 7

    def piece_copy(r, s, c):
        slot = lax.rem(y + 8 * (s - 1) - way(r) * (s - 1), NY)
        return pltpu.make_async_remote_copy(
            src_ref=piece.at[slot, chunk(c)], dst_ref=piece.at[slot, chunk(c)],
            send_sem=piece_send, recv_sem=piece_recv.at[r, s, c],
            device_id=y_peer(way(r)), device_id_type=MESH)

    def unit_copy(r, s, c):
        slot = lax.rem(z + 8 * (s - 1) - way(r) * (s - 1), NZ)
        return pltpu.make_async_remote_copy(
            src_ref=unit.at[slot, half_chunk(c)], dst_ref=unit.at[slot, half_chunk(c)],
            send_sem=unit_send, recv_sem=unit_recv.at[r, s, c],
            device_id=z_peer(way(r)), device_id_type=MESH)

    def core_copy(r, s, c):
        slot = lax.rem(z + 8 * s - way(r) * s, NZ)
        return pltpu.make_async_remote_copy(
            src_ref=unit.at[slot, half_chunk(c)], dst_ref=unit.at[slot, half_chunk(c)],
            send_sem=core_send, recv_sem=core_recv.at[r, s, c],
            device_id=other_core, device_id_type=MESH)

    for c in range(CHUNKS):
        for r in range(2):
            unit_copy(r, 1, c).start()
            piece_copy(r, 1, c).start()

    def slot_pair(t):
        k = sum((t >= j * j).astype(jnp.int32) for j in range(1, 8))
        rest = t - k * k
        ku = jnp.where(rest <= k, k, rest - k - 1)
        kv = jnp.where(rest <= k, rest, k)
        return lax.rem(z - near_first(ku) + NZ, NZ), lax.rem(y - near_first(kv) + NY, NY)

    def four(b, _):
        for q in range(4):
            us, vs = slot_pair(4 * b + q)
            e = jnp.exp2(jnp.dot(unit[us], piece[vs], preferred_element_type=F32) * scale[vs])
            tile[vs, pl.ds(pl.multiple_of(us * ROWS, ROWS), ROWS), :] = e
            colacc[vs] += jnp.sum(e.reshape(ROWS // 8, 8, COLS), axis=0)
        return 0

    def arrive(s, _):
        for c in range(CHUNKS):
            for r in range(2):
                @pl.when(s + r <= 4)
                def _():
                    unit_copy(r, s, c).wait_recv()
                    core_copy(r, s, c).start()

                    @pl.when(s + r < 4)
                    def _():
                        unit_copy(r, s + 1, c).start()

                    piece_copy(r, s, c).wait_recv()

                    @pl.when(s + r < 4)
                    def _():
                        piece_copy(r, s + 1, c).start()

        set_scale(lax.rem(y + 7 * s, NY))

        @pl.when(s < 4)
        def _():
            set_scale(lax.rem(y + s, NY))

        for c in range(CHUNKS):
            for r in range(2):
                @pl.when(s + r <= 4)
                def _():
                    core_copy(r, s, c).wait_recv()

        before = 2 * s - 1
        now = jnp.minimum(2 * s + 1, 8)
        lax.fori_loop(before * before // 4, now * now // 4, four, 0)
        return 0

    lax.fori_loop(1, 5, arrive, 0)

    def col_copy(step, d):
        return pltpu.make_async_remote_copy(
            src_ref=colbuf.at[step, 0], dst_ref=colbuf.at[step, d],
            send_sem=col_send.at[step], recv_sem=col_recv.at[step],
            device_id=y_peer(d), device_id_type=MESH)

    def rowp_copy(step, h, d):
        part = pl.ds(h * PART, PART)
        return pltpu.make_async_remote_copy(
            src_ref=rowpart.at[part], dst_ref=rowbuf.at[step, h, d],
            send_sem=rowp_send.at[step], recv_sem=rowp_recv.at[step, h],
            device_id=p_peer(d), device_id_type=MESH)

    def rowz_copy(step, h, d):
        return pltpu.make_async_remote_copy(
            src_ref=rowall.at[step, h, 0], dst_ref=rowall.at[step, h, d],
            send_sem=rowz_send.at[step], recv_sem=rowz_recv.at[step, h],
            device_id=z_peer(d), device_id_type=MESH)

    def lastz_copy(d):
        return pltpu.make_async_remote_copy(
            src_ref=rowpart.at[lax.rem(z + d, NZ)], dst_ref=lastz.at[d],
            send_sem=rowz_send.at[ITERS - 1], recv_sem=rowz_recv.at[ITERS - 1, 0],
            device_id=z_peer(d), device_id_type=MESH)

    def lastp_copy(d):
        return pltpu.make_async_remote_copy(
            src_ref=lastp.at[me_p], dst_ref=lastp.at[me_p],
            send_sem=rowp_send.at[ITERS - 1], recv_sem=rowp_recv.at[ITERS - 1, 0],
            device_id=p_peer(d), device_id_type=MESH)

    def settle(ref, semaphore):
        pltpu.make_async_copy(ref, ref, semaphore).wait()

    def send_all(copy):
        for d in FAR_FIRST:
            copy(d).start()

    def rows_of(i, q):
        return pl.ds(pl.multiple_of(i * BLOCK + q * LANES, LANES), LANES)

    def column_pass(step):
        def spread(i):
            return [jnp.broadcast_to(weight[i, q:q + 1, :], (LANES, LANES)).T for q in range(PER)]

        def part_pass(h, acc):
            settle(rowall.at[step, h, 1:], rowz_recv.at[step, h])
            weight[pl.ds(h * PART, PART)] = 1.0 / (IMAGES * jnp.sum(rowall[step, h], axis=0))
            first = h * PART
            for q, w in enumerate(spread(first)):
                wide[0, q] = w

            def body(i, acc):
                acc = list(acc)
                ws = [wide[lax.rem(i, 2), q] for q in range(PER)]
                ahead = spread(first + jnp.minimum(i + 1, PART - 1))
                for q in range(PER):
                    for j in range(2 * NY):
                        t = tile[j // 2, rows_of(first + i, q), (j % 2) * LANES:(j % 2 + 1) * LANES] * ws[q]
                        acc[j] = acc[j] + jnp.sum(t.reshape(LANES // 8, 8, LANES), axis=0)
                for q in range(PER):
                    wide[1 - lax.rem(i, 2), q] = ahead[q]
                return tuple(acc)

            return lax.fori_loop(0, PART, body, acc)

        acc = lax.fori_loop(0, SPLIT, part_pass, tuple(jnp.zeros((8, LANES), F32) for _ in range(2 * NY)))
        for j in range(2 * NY):
            colacc[j // 2, :, (j % 2) * LANES:(j % 2 + 1) * LANES] = acc[j]

    def row_pass(slot, done):
        def work(i):
            out = []
            for q in range(PER):
                acc = None
                for j in range(2 * NY):
                    lanes = slice((j % 2) * LANES, (j % 2 + 1) * LANES)
                    t = tile[j // 2, rows_of(slot(i), q), lanes] * colval[j // 2:j // 2 + 1, lanes]
                    acc = t if acc is None else acc + t
                out.append(acc)
            return out

        def finish(i):
            return [jnp.sum(wide[lax.rem(i, 2), q].T, axis=0, keepdims=True) for q in range(PER)]

        def put(i, sums):
            for q in range(PER):
                rowpart[slot(i), q:q + 1, :] = sums[q]

        for q, part in enumerate(work(0)):
            wide[0, q] = part

        def body(i, _):
            sums = finish(i - 1)
            parts = work(i)
            put(i - 1, sums)
            for q in range(PER):
                wide[lax.rem(i, 2), q] = parts[q]
            done(i - 1)
            return 0

        lax.fori_loop(1, NBLOCK, body, 0)
        put(NBLOCK - 1, finish(NBLOCK - 1))
        done(NBLOCK - 1)

    for step in range(ITERS):
        if step > 0:
            column_pass(step - 1)
        colbuf[step, 0] = jnp.sum(colacc[...], axis=1)
        send_all(lambda d: col_copy(step, d))
        settle(colbuf.at[step, 1:], col_recv.at[step])
        colval[...] = 1.0 / (K * jnp.sum(colbuf[step], axis=0))
        if step < ITERS - 1:
            def send_part(i):
                @pl.when(lax.rem(i, PART) == PART - 1)
                def _():
                    send_all(lambda d: rowp_copy(step, i // PART, d))

            row_pass(lambda i: i, send_part)

            def sum_part(h, _):
                settle(rowbuf.at[step, h, 1:], rowp_recv.at[step, h])
                rowall[step, h, 0] = rowpart[pl.ds(h * PART, PART)] + jnp.sum(rowbuf[step, h, 1:], axis=0)
                send_all(lambda d: rowz_copy(step, h, d))
                return 0

            lax.fori_loop(0, SPLIT, sum_part, 0)
            settle(rowbuf.at[step, :, 1:], rowp_send.at[step])
        else:
            def distance(i):
                return near_first(NBLOCK - 1 - i)

            def send_one(i):
                @pl.when(i < NBLOCK - 1)
                def _():
                    lastz_copy(distance(i)).start()

            row_pass(lambda i: lax.rem(z + distance(i), NZ), send_one)
            settle(lastz.at[1:], rowz_recv.at[ITERS - 1, 0])
            lastp[pl.ds(me_p, 1)] = rowpart[pl.ds(z, 1)] + jnp.sum(lastz[1:], axis=0)[None]
            send_all(lastp_copy)
            settle(lastp.at[1:], rowp_recv.at[ITERS - 1, 0])
            row_out[...] = IMAGES * (1.0 / (IMAGES * jnp.sum(lastp[...], axis=0)))
            col_out[...] = float(K) * float(IMAGES) * colval[pl.ds(y, 1), :]

    settle(unit.at[1:, pl.ds(0, HALF)], unit_send)
    settle(unit.at[1:, pl.ds(0, HALF)], core_send)
    settle(piece.at[1:], piece_send)
    for step in range(ITERS):
        settle(colbuf.at[step, 1:], col_send.at[step])
    for step in range(ITERS - 1):
        settle(rowall.at[step, :, 1:], rowz_send.at[step])
    settle(lastz.at[1:], rowz_send.at[ITERS - 1])
    settle(lastp.at[1:], rowp_send.at[ITERS - 1])


def local(features, prototypes):
    vmem = pl.BlockSpec(memory_space=pltpu.VMEM)
    row_mass, col_mass = pl.pallas_call(
        kernel,
        out_shape=(
            jax.ShapeDtypeStruct((ROWS // LANES, LANES), F32),
            jax.ShapeDtypeStruct((1, COLS), F32),
        ),
        in_specs=[vmem, vmem],
        out_specs=(vmem, vmem),
        scratch_shapes=[
            pltpu.VMEM((NY, NZ * ROWS, COLS), F32),
            pltpu.VMEM((NZ, ROWS, 256), BF16),
            pltpu.VMEM((NY, 256, COLS), BF16),
            pltpu.VMEM((NY, 1, COLS), F32),
            pltpu.VMEM((NY, 8, COLS), F32),
            pltpu.VMEM((ITERS, NY, NY, COLS), F32),
            pltpu.VMEM((NY, COLS), F32),
            pltpu.VMEM((NZ, 4, LANES), F32),
            pltpu.VMEM((ITERS - 1, SPLIT, NP, PART, 4, LANES), F32),
            pltpu.VMEM((ITERS - 1, SPLIT, NZ, PART, 4, LANES), F32),
            pltpu.VMEM((NZ, 4, LANES), F32),
            pltpu.VMEM((NP, 4, LANES), F32),
            pltpu.VMEM((NZ, 4, LANES), F32),
            pltpu.VMEM((2, PER, LANES, LANES), F32),
        ]
        + [pltpu.SemaphoreType.DMA, pltpu.SemaphoreType.DMA((2, 5, CHUNKS))] * 3
        + [pltpu.SemaphoreType.DMA((ITERS,))] * 2
        + [pltpu.SemaphoreType.DMA((ITERS,)), pltpu.SemaphoreType.DMA((ITERS, SPLIT))] * 2,
        compiler_params=pltpu.CompilerParams(
            collective_id=0, has_side_effects=True, vmem_limit_bytes=56 * 2**20
        ),
        cost_estimate=pl.CostEstimate(
            flops=2 * 4096 * 2048 * 256, bytes_accessed=2**20, transcendentals=4096 * 2048
        ),
        name="sinkhorn",
    )(features, prototypes)
    return jnp.log(row_mass.reshape(ROWS)), jnp.log(col_mass.reshape(COLS))


def solution(mesh):
    in_specs = (P("dp", None), P(None, ("proto", "dp")))
    out_specs = (P("dp"), P(("proto", "dp")))
    return jax.shard_map(local, mesh=mesh, in_specs=in_specs, out_specs=out_specs, check_vma=False)
```

time: 98.3 us -> 89.5 us (0.910)
  Pallas kernels: 95.6 us -> 86.8 us
    pallas_call x1, Pallas kernels: 95.6 us -> 86.8 us  [local(): pl.pallas_call(kernel, out_shape=(jax.ShapeDtypeStruct((ROWS // LANES, LA...]
    log x0 -> x2, local copies, waits for them, and re-layouts: none -> 1.16 us  [local(): return (jnp.log(row_mass.reshape(ROWS)), jnp.log(col_mass.reshape(COLS)))]
    unnamed x6 -> x4, local copies, waits for them, and re-layouts: 1.86 us -> 0.71 us
where the time goes in v3:
time: 89.5 us; the launch traced here: 89.3 us
  Pallas kernels  86.8 us (97%)
  local copies, waits for them, and re-layouts  1.86 us (2%)
    pallas_call x1, Pallas kernels, local(): pl.pallas_call(kernel, out_shape=(jax.ShapeDtypeStruct((ROWS // LANES, LA...  86.8 us

profile of v3, /device:TPU:1, one launch (start us, length us, event | category | flops | bytes accessed | tf_op | source)
XLA Modules:
  0.0 89.3 jit_solution(16597625526399439933)
XLA Ops:
  0.6 86.8 %sinkhorn.1 = (f32[4,128]{1,0:T(4,128)}, f32[1,256]{1,0:T(1,128)}) custom-call(bf16[512,256]{1,0:T(8,128)(2,1)} %feat.1, bf16[256,256]{1,0:T(8,128)(2,1)} %proto.1), custom_call_target="tpu_custom_call" | custom-call | flops 4294967296 | bytes 1048576 | tf_op jit(solution)/shard_map/sinkhorn/pallas_call | solution.py:328
  87.4 0.0 copy-start
  87.4 0.7 copy-done
  88.1 0.0 copy-start.1
  88.1 0.6 log_bitcast_fusion
  88.7 0.0 copy-done.1
  88.7 0.6 log.14
Async XLA Ops:
  87.4 0.7 copy-start
  88.1 0.6 copy-start.1

commit v4 on v3

--- a/solution.py
+++ b/solution.py
@@ -15,6 +15,7 @@
 COLS = 256
 HALF = ROWS // 2
 CHUNKS = 2
+GROUP = 8
 SPLIT = 4
 PART = NZ // SPLIT
 FAR_FIRST = (4, 3, 5, 2, 6, 1, 7)
@@ -36,8 +37,8 @@
 
 def kernel(
     feat, proto, row_out, col_out,
-    tile, unit, piece, scale, colacc, colbuf, colval, rowpart, rowbuf, rowall, lastz, lastp, weight, wide,
-    unit_send, unit_recv, core_send, core_recv, piece_send, piece_recv,
+    images, tile, unit, piece, scale, colacc, colbuf, colval, rowpart, rowbuf, rowall, lastz, lastp, weight, wide,
+    in_sem, unit_send, unit_recv, core_send, core_recv, piece_send, piece_recv,
     col_send, col_recv, rowp_send, rowp_recv, rowz_send, rowz_recv,
 ):
     dp = lax.axis_index("dp")
@@ -59,25 +60,29 @@
     barrier = pltpu.get_barrier_semaphore()
 
     def greet(d, _):
+        pl.semaphore_signal(barrier, inc=1, device_id=p_peer(d), device_id_type=MESH)
+        return 0
+
+    for d in (1, 7):
         pl.semaphore_signal(barrier, inc=1, device_id=y_peer(d), device_id_type=MESH)
         pl.semaphore_signal(barrier, inc=1, device_id=z_peer(d), device_id_type=MESH)
-        pl.semaphore_signal(barrier, inc=1, device_id=p_peer(d), device_id_type=MESH)
-        return 0
-
     lax.fori_loop(1, 8, greet, 0)
 
-    values = feat[...].astype(F32)
-    norm = jnp.sqrt(jnp.sum(values * values, axis=1, keepdims=True) + EPS)
-    unit[pl.ds(z, 1)] = (values / norm).astype(BF16)[None]
-    piece[pl.ds(y, 1)] = proto[...][None]
-    colacc[...] = jnp.zeros_like(colacc)
+    def set_unit(rows):
+        values = images[rows, :].astype(F32)
+        norm = jnp.sqrt(jnp.sum(values * values, axis=1, keepdims=True) + EPS)
+        unit[z, rows, :] = (values / norm).astype(BF16)
 
     def set_scale(vs):
         v = piece[vs].astype(F32)
         scale[vs] = (LOG2E / SHARP) / jnp.sqrt(jnp.sum(v * v, axis=0, keepdims=True) + EPS)
 
-    set_scale(y)
-    pl.semaphore_wait(barrier, 21)
+    proto_copy = pltpu.make_async_copy(proto, piece.at[y], in_sem.at[0])
+    feat_copy = pltpu.make_async_copy(feat, images, in_sem.at[1])
+    proto_copy.start()
+    feat_copy.start()
+    proto_copy.wait()
+    pl.semaphore_wait(barrier, 11)
 
     def chunk(c):
         return pl.ds(c * (256 // CHUNKS), 256 // CHUNKS)
@@ -112,60 +117,72 @@
 
     for c in range(CHUNKS):
         for r in range(2):
+            piece_copy(r, 1, c).start()
+    feat_copy.wait()
+    set_unit(pl.ds(pl.multiple_of(core * HALF, HALF), HALF))
+    for c in range(CHUNKS):
+        for r in range(2):
             unit_copy(r, 1, c).start()
-            piece_copy(r, 1, c).start()
+    set_unit(pl.ds(pl.multiple_of((1 - core) * HALF, HALF), HALF))
+    set_scale(y)
+    colacc[...] = jnp.zeros_like(colacc)
+    wide[...] = jnp.zeros_like(wide)
 
     def slot_pair(t):
         k = sum((t >= j * j).astype(jnp.int32) for j in range(1, 8))
         rest = t - k * k
-        ku = jnp.where(rest <= k, k, rest - k - 1)
-        kv = jnp.where(rest <= k, rest, k)
+        ku = jnp.where(rest < k, rest, k)
+        kv = jnp.where(rest < k, k, rest - k)
         return lax.rem(z - near_first(ku) + NZ, NZ), lax.rem(y - near_first(kv) + NY, NY)
 
-    def four(b, _):
-        for q in range(4):
-            us, vs = slot_pair(4 * b + q)
+    def blocks(b, _):
+        for q in range(GROUP):
+            us, vs = slot_pair(GROUP * b + q)
             e = jnp.exp2(jnp.dot(unit[us], piece[vs], preferred_element_type=F32) * scale[vs])
             tile[vs, pl.ds(pl.multiple_of(us * ROWS, ROWS), ROWS), :] = e
             colacc[vs] += jnp.sum(e.reshape(ROWS // 8, 8, COLS), axis=0)
         return 0
 
+    def last_block(s):
+        return s + (s >= 2).astype(jnp.int32) + 2 * (s >= 3).astype(jnp.int32)
+
     def arrive(s, _):
         for c in range(CHUNKS):
             for r in range(2):
+                for copy in (piece_copy, unit_copy):
+                    @pl.when(s + r <= 4)
+                    def _():
+                        copy(r, s, c).wait_recv()
+
+                        @pl.when(s + r < 4)
+                        def _():
+                            copy(r, s + 1, c).start()
+
+            for r in range(2):
                 @pl.when(s + r <= 4)
                 def _():
-                    unit_copy(r, s, c).wait_recv()
                     core_copy(r, s, c).start()
 
-                    @pl.when(s + r < 4)
-                    def _():
-                        unit_copy(r, s + 1, c).start()
-
-                    piece_copy(r, s, c).wait_recv()
-
-                    @pl.when(s + r < 4)
-                    def _():
-                        piece_copy(r, s + 1, c).start()
-
-        set_scale(lax.rem(y + 7 * s, NY))
+        @pl.when(s <= 4)
+        def _():
+            set_scale(lax.rem(y + 7 * s, NY))
 
         @pl.when(s < 4)
         def _():
             set_scale(lax.rem(y + s, NY))
-
-        for c in range(CHUNKS):
-            for r in range(2):
-                @pl.when(s + r <= 4)
-                def _():
+            for c in range(CHUNKS):
+                for r in range(2):
                     core_copy(r, s, c).wait_recv()
 
-        before = 2 * s - 1
-        now = jnp.minimum(2 * s + 1, 8)
-        lax.fori_loop(before * before // 4, now * now // 4, four, 0)
+        @pl.when(s == 5)
+        def _():
+            for c in range(CHUNKS):
+                core_copy(0, 4, c).wait_recv()
+
+        lax.fori_loop(last_block(s - 1), last_block(s), blocks, 0)
         return 0
 
-    lax.fori_loop(1, 5, arrive, 0)
+    lax.fori_loop(1, 6, arrive, 0)
 
     def col_copy(step, d):
         return pltpu.make_async_remote_copy(
@@ -256,37 +273,59 @@
             for q in range(PER):
                 rowpart[slot(i), q:q + 1, :] = sums[q]
 
-        for q, part in enumerate(work(0)):
-            wide[0, q] = part
-
-        def body(i, _):
-            sums = finish(i - 1)
-            parts = work(i)
-            put(i - 1, sums)
+        def store(i, parts):
             for q in range(PER):
                 wide[lax.rem(i, 2), q] = parts[q]
-            done(i - 1)
+
+        def body(i, _):
+            before = jnp.maximum(i - 1, 0)
+            sums = finish(i + 1)
+            parts = work(i)
+            put(before, sums)
+            store(i, parts)
+
+            @pl.when((i > 0) & (lax.rem(i, PART) == 0))
+            def _():
+                done(i // PART - 1)
+
             return 0
 
-        lax.fori_loop(1, NBLOCK, body, 0)
+        lax.fori_loop(0, NBLOCK, body, 0)
         put(NBLOCK - 1, finish(NBLOCK - 1))
-        done(NBLOCK - 1)
-
-    for step in range(ITERS):
-        if step > 0:
+        done(SPLIT - 1)
+
+    def distance(i):
+        return near_first(NBLOCK - 1 - i)
+
+    def iteration(step, _):
+        last = step == ITERS - 1
+
+        @pl.when(step > 0)
+        def _():
             column_pass(step - 1)
+
         colbuf[step, 0] = jnp.sum(colacc[...], axis=1)
         send_all(lambda d: col_copy(step, d))
         settle(colbuf.at[step, 1:], col_recv.at[step])
         colval[...] = 1.0 / (K * jnp.sum(colbuf[step], axis=0))
-        if step < ITERS - 1:
-            def send_part(i):
-                @pl.when(lax.rem(i, PART) == PART - 1)
+
+        def send_part(h):
+            @pl.when(jnp.logical_not(last))
+            def _():
+                send_all(lambda d: rowp_copy(step, h, d))
+
+            @pl.when(last)
+            def _():
+                lastz_copy(distance(2 * h)).start()
+
+                @pl.when(h < SPLIT - 1)
                 def _():
-                    send_all(lambda d: rowp_copy(step, i // PART, d))
-
-            row_pass(lambda i: i, send_part)
-
+                    lastz_copy(distance(2 * h + 1)).start()
+
+        row_pass(lambda i: jnp.where(last, lax.rem(z + distance(i), NZ), i), send_part)
+
+        @pl.when(jnp.logical_not(last))
+        def _():
             def sum_part(h, _):
                 settle(rowbuf.at[step, h, 1:], rowp_recv.at[step, h])
                 rowall[step, h, 0] = rowpart[pl.ds(h * PART, PART)] + jnp.sum(rowbuf[step, h, 1:], axis=0)
@@ -295,22 +334,16 @@
 
             lax.fori_loop(0, SPLIT, sum_part, 0)
             settle(rowbuf.at[step, :, 1:], rowp_send.at[step])
-        else:
-            def distance(i):
-                return near_first(NBLOCK - 1 - i)
-
-            def send_one(i):
-                @pl.when(i < NBLOCK - 1)
-                def _():
-                    lastz_copy(distance(i)).start()
-
-            row_pass(lambda i: lax.rem(z + distance(i), NZ), send_one)
-            settle(lastz.at[1:], rowz_recv.at[ITERS - 1, 0])
-            lastp[pl.ds(me_p, 1)] = rowpart[pl.ds(z, 1)] + jnp.sum(lastz[1:], axis=0)[None]
-            send_all(lastp_copy)
-            settle(lastp.at[1:], rowp_recv.at[ITERS - 1, 0])
-            row_out[...] = IMAGES * (1.0 / (IMAGES * jnp.sum(lastp[...], axis=0)))
-            col_out[...] = float(K) * float(IMAGES) * colval[pl.ds(y, 1), :]
+
+        return 0
+
+    lax.fori_loop(0, ITERS, iteration, 0)
+    settle(lastz.at[1:], rowz_recv.at[ITERS - 1, 0])
+    lastp[pl.ds(me_p, 1)] = rowpart[pl.ds(z, 1)] + jnp.sum(lastz[1:], axis=0)[None]
+    send_all(lastp_copy)
+    settle(lastp.at[1:], rowp_recv.at[ITERS - 1, 0])
+    row_out[...] = IMAGES * (1.0 / (IMAGES * jnp.sum(lastp[...], axis=0)))
+    col_out[...] = float(K) * float(IMAGES) * colval[pl.ds(y, 1), :]
 
     settle(unit.at[1:, pl.ds(0, HALF)], unit_send)
     settle(unit.at[1:, pl.ds(0, HALF)], core_send)
@@ -331,9 +364,10 @@
             jax.ShapeDtypeStruct((ROWS // LANES, LANES), F32),
             jax.ShapeDtypeStruct((1, COLS), F32),
         ),
-        in_specs=[vmem, vmem],
+        in_specs=[pl.BlockSpec(memory_space=pltpu.HBM)] * 2,
         out_specs=(vmem, vmem),
         scratch_shapes=[
+            pltpu.VMEM((ROWS, 256), BF16),
             pltpu.VMEM((NY, NZ * ROWS, COLS), F32),
             pltpu.VMEM((NZ, ROWS, 256), BF16),
             pltpu.VMEM((NY, 256, COLS), BF16),
@@ -349,11 +383,12 @@
             pltpu.VMEM((NZ, 4, LANES), F32),
             pltpu.VMEM((2, PER, LANES, LANES), F32),
         ]
+        + [pltpu.SemaphoreType.DMA((2,))]
         + [pltpu.SemaphoreType.DMA, pltpu.SemaphoreType.DMA((2, 5, CHUNKS))] * 3
         + [pltpu.SemaphoreType.DMA((ITERS,))] * 2
         + [pltpu.SemaphoreType.DMA((ITERS,)), pltpu.SemaphoreType.DMA((ITERS, SPLIT))] * 2,
         compiler_params=pltpu.CompilerParams(
-            collective_id=0, has_side_effects=True, vmem_limit_bytes=56 * 2**20
+            collective_id=0, has_side_effects=True, vmem_limit_bytes=40 * 2**20
         ),
         cost_estimate=pl.CostEstimate(
             flops=2 * 4096 * 2048 * 256, bytes_accessed=2**20, transcendentals=4096 * 2048

time: 89.5 us -> 87.1 us (0.973)
  Pallas kernels: 86.8 us -> 83.3 us
  local copies, waits for them, and re-layouts: 1.86 us -> 3 us
    pallas_call x1, Pallas kernels: 86.8 us -> 83.3 us  [local(): pl.pallas_call(kernel, out_shape=(jax.ShapeDtypeStruct((ROWS // LANES, LA...]
    unnamed x4, local copies, waits for them, and re-layouts: 0.71 us -> 1.85 us
where the time goes in v4:
time: 87.1 us; the launch traced here: 87 us
  Pallas kernels  83.3 us (96%)
  local copies, waits for them, and re-layouts  3 us (3%)
    pallas_call x1, Pallas kernels, local(): pl.pallas_call(kernel, out_shape=(jax.ShapeDtypeStruct((ROWS // LANES, LA...  83.3 us
    unnamed x4, local copies, waits for them, and re-layouts  1.85 us

profile of v4, /device:TPU:1, one launch (start us, length us, event | category | flops | bytes accessed | tf_op | source)
XLA Modules:
  0.0 87.0 jit_solution(875547971745049705)
XLA Ops:
  0.6 0.0 copy-start
  0.6 0.9 %copy-done = bf16[512,256]{1,0:T(8,128)(2,1)S(1)} copy-done((bf16[512,256]{1,0:T(8,128)(2,1)S(1)}, bf16[512,256]{1,0:T(8,128)(2,1)}, u32[]{:S(2)}) %copy-start) | copy-done | bytes 262168
  1.6 0.0 copy-start.1
  1.6 0.9 %copy-done.1 = bf16[256,256]{1,0:T(8,128)(2,1)S(1)} copy-done((bf16[256,256]{1,0:T(8,128)(2,1)S(1)}, bf16[256,256]{1,0:T(8,128)(2,1)}, u32[]{:S(2)}) %copy-start.1) | copy-done | bytes 131096
  2.5 83.3 %sinkhorn.1 = (f32[4,128]{1,0:T(4,128)S(1)}, f32[1,256]{1,0:T(1,128)S(1)}) custom-call(bf16[512,256]{1,0:T(8,128)(2,1)S(1)} %copy-done, bf16[256,256]{1,0:T(8,128)(2,1)S(1)} %copy-done.1), custom_call_target="tpu_custom_call" | custom-call | flops 4294967296 | bytes 1048576 | tf_op jit(solution)/shard_map/sinkhorn/pallas_call | solution.py:361
  85.8 0.6 log_bitcast_fusion
  86.4 0.6 log.14
Async XLA Ops:
  0.6 1.0 %copy-start = (bf16[512,256]{1,0:T(8,128)(2,1)S(1)}, bf16[512,256]{1,0:T(8,128)(2,1)}, u32[]{:S(2)}) copy-start(bf16[512,256]{1,0:T(8,128)(2,1)} %feat.1) | copy-start | bytes 786436
  1.6 0.9 %copy-start.1 = (bf16[256,256]{1,0:T(8,128)(2,1)S(1)}, bf16[256,256]{1,0:T(8,128)(2,1)}, u32[]{:S(2)}) copy-start(bf16[256,256]{1,0:T(8,128)(2,1)} %proto.1) | copy-start | bytes 393220

commit v5 on v4

--- a/solution.py
+++ b/solution.py
@@ -354,6 +354,11 @@
         settle(rowall.at[step, :, 1:], rowz_send.at[step])
     settle(lastz.at[1:], rowz_send.at[ITERS - 1])
     settle(lastp.at[1:], rowp_send.at[ITERS - 1])
+
+
+def logs(row_mass, col_mass, row_log, col_log):
+    row_log[...] = jnp.log(row_mass[...])
+    col_log[...] = jnp.log(col_mass[...])
 
 
 def local(features, prototypes):
@@ -388,14 +393,24 @@
         + [pltpu.SemaphoreType.DMA((ITERS,))] * 2
         + [pltpu.SemaphoreType.DMA((ITERS,)), pltpu.SemaphoreType.DMA((ITERS, SPLIT))] * 2,
         compiler_params=pltpu.CompilerParams(
-            collective_id=0, has_side_effects=True, vmem_limit_bytes=40 * 2**20
+            collective_id=0, has_side_effects=True, vmem_limit_bytes=56 * 2**20
         ),
         cost_estimate=pl.CostEstimate(
             flops=2 * 4096 * 2048 * 256, bytes_accessed=2**20, transcendentals=4096 * 2048
         ),
         name="sinkhorn",
     )(features, prototypes)
-    return jnp.log(row_mass.reshape(ROWS)), jnp.log(col_mass.reshape(COLS))
+    row_log, col_log = pl.pallas_call(
+        logs,
+        out_shape=(
+            jax.ShapeDtypeStruct((ROWS // LANES, LANES), F32),
+            jax.ShapeDtypeStruct((1, COLS), F32),
+        ),
+        in_specs=[vmem, vmem],
+        out_specs=(vmem, vmem),
+        name="logs",
+    )(row_mass, col_mass)
+    return row_log.reshape(ROWS), col_log.reshape(COLS)
 
 
 def solution(mesh):

time: 87.1 us -> 85.9 us (0.986)
  local copies, waits for them, and re-layouts: 3 us -> 0 us
  Pallas kernels: 83.3 us -> 85.1 us
    unnamed x4 -> x0, local copies, waits for them, and re-layouts: 1.85 us -> none
    pallas_call x0 -> x1, Pallas kernels: none -> 1.26 us  [local(): pl.pallas_call(logs, out_shape=(jax.ShapeDtypeStruct((ROWS // LANES, LANE...]
    log x2 -> x0, local copies, waits for them, and re-layouts: 1.16 us -> none  [local(): return (jnp.log(row_mass.reshape(ROWS)), jnp.log(col_mass.reshape(COLS)))]
where the time goes in v5:
time: 85.9 us; the launch traced here: 85.8 us
  Pallas kernels  85.1 us (99%)
    pallas_call x1, Pallas kernels, local(): pl.pallas_call(kernel, out_shape=(jax.ShapeDtypeStruct((ROWS // LANES, LA...  83.9 us

profile of v5, /device:TPU:1, one launch (start us, length us, event | category | flops | bytes accessed | tf_op | source)
XLA Modules:
  0.0 85.8 jit_solution(8534688990725545190)
XLA Ops:
  0.6 83.9 %sinkhorn.1 = (f32[4,128]{1,0:T(4,128)}, f32[1,256]{1,0:T(1,128)}) custom-call(bf16[512,256]{1,0:T(8,128)(2,1)} %feat.1, bf16[256,256]{1,0:T(8,128)(2,1)} %proto.1), custom_call_target="tpu_custom_call" | custom-call | flops 4294967296 | bytes 1048576 | tf_op jit(solution)/shard_map/sinkhorn/pallas_call | solution.py:366
  84.5 1.3 %logs.1 = (f32[4,128]{1,0:T(4,128)}, f32[1,256]{1,0:T(1,128)}) custom-call(f32[4,128]{1,0:T(4,128)} %get-tuple-element.6.row_mass, f32[1,256]{1,0:T(1,128)} %get-tuple-element.7.col_mass), custom_call_target="tpu_custom_call" | custom-call | tf_op jit(solution)/shard_map/logs/pallas_call | solution.py:403

commit v6 on v5

--- a/solution.py
+++ b/solution.py
@@ -16,7 +16,7 @@
 HALF = ROWS // 2
 CHUNKS = 2
 GROUP = 8
-SPLIT = 4
+SPLIT = 8
 PART = NZ // SPLIT
 FAR_FIRST = (4, 3, 5, 2, 6, 1, 7)
 BLOCK = 512
@@ -239,13 +239,13 @@
             def body(i, acc):
                 acc = list(acc)
                 ws = [wide[lax.rem(i, 2), q] for q in range(PER)]
-                ahead = spread(first + jnp.minimum(i + 1, PART - 1))
+                ahead = spread(first + jnp.minimum(i + 1, PART - 1)) if PART > 1 else []
                 for q in range(PER):
                     for j in range(2 * NY):
                         t = tile[j // 2, rows_of(first + i, q), (j % 2) * LANES:(j % 2 + 1) * LANES] * ws[q]
                         acc[j] = acc[j] + jnp.sum(t.reshape(LANES // 8, 8, LANES), axis=0)
-                for q in range(PER):
-                    wide[1 - lax.rem(i, 2), q] = ahead[q]
+                for q, w in enumerate(ahead):
+                    wide[1 - lax.rem(i, 2), q] = w
                 return tuple(acc)
 
             return lax.fori_loop(0, PART, body, acc)
@@ -316,11 +316,10 @@
 
             @pl.when(last)
             def _():
-                lastz_copy(distance(2 * h)).start()
-
-                @pl.when(h < SPLIT - 1)
-                def _():
-                    lastz_copy(distance(2 * h + 1)).start()
+                for j in range(PART):
+                    @pl.when(h * PART + j < NBLOCK - 1)
+                    def _():
+                        lastz_copy(distance(h * PART + j)).start()
 
         row_pass(lambda i: jnp.where(last, lax.rem(z + distance(i), NZ), i), send_part)
 

time: 85.9 us -> 85 us (0.990)
  Pallas kernels: 85.1 us -> 84.2 us
    pallas_call x1, Pallas kernels: 83.9 us -> 83 us  [local(): pl.pallas_call(kernel, out_shape=(jax.ShapeDtypeStruct((ROWS // LANES, LA...]
where the time goes in v6:
time: 85 us; the launch traced here: 84.9 us
  Pallas kernels  84.2 us (99%)
    pallas_call x1, Pallas kernels, local(): pl.pallas_call(kernel, out_shape=(jax.ShapeDtypeStruct((ROWS // LANES, LA...  83 us

profile of v6, /device:TPU:1, one launch (start us, length us, event | category | flops | bytes accessed | tf_op | source)
XLA Modules:
  0.0 84.9 jit_solution(201751897039789489)
XLA Ops:
  0.6 83.0 %sinkhorn.1 = (f32[4,128]{1,0:T(4,128)}, f32[1,256]{1,0:T(1,128)}) custom-call(bf16[512,256]{1,0:T(8,128)(2,1)} %feat.1, bf16[256,256]{1,0:T(8,128)(2,1)} %proto.1), custom_call_target="tpu_custom_call" | custom-call | flops 4294967296 | bytes 1048576 | tf_op jit(solution)/shard_map/sinkhorn/pallas_call | solution.py:365
  83.6 1.3 %logs.1 = (f32[4,128]{1,0:T(4,128)}, f32[1,256]{1,0:T(1,128)}) custom-call(f32[4,128]{1,0:T(4,128)} %get-tuple-element.6.row_mass, f32[1,256]{1,0:T(1,128)} %get-tuple-element.7.col_mass), custom_call_target="tpu_custom_call" | custom-call | tf_op jit(solution)/shard_map/logs/pallas_call | solution.py:402
